TPU v7x, 1024 devices: a whole 4x4x32 slice. The times are simulated.
1024 devices in a mesh: gx: 8 (over z_lo), gy: 64 (over z_hi, y, x), gz: 2 (over core).
Axes of the slice: x: 4, y: 4, z: 32 (z_hi: 4, z_lo: 8; z = z_hi * 8 + z_lo), core: 2. Of those that a mesh axis runs over, the one named last changes fastest.
Arguments:
- density: float32 [32, 512, 256], P('gx', 'gy', 'gz'), may hold values from 0.5 to 2
- velocity: float32 [3, 32, 512, 256], P(None, 'gx', 'gy', 'gz'), may hold values from -0.5 to 0.5
- magnetic: float32 [3, 32, 512, 256], P(None, 'gx', 'gy', 'gz'), may hold values from -1 to 1
- concentration: float32 [32, 512, 256], P('gx', 'gy', 'gz'), may hold values from 0 to 1
- shear_cells: int32 [2], replicated, may hold values from 0 to 511
- shear_frac: float32 [2], replicated, may hold values from 0 to 1
Outputs:
- evolved: float32 [8, 32, 512, 256], P(None, 'gx', 'gy', 'gz')
All inputs are finite; a program needn't handle non-finite values.
Results may differ from a plain program's by a relative error of at most 0.0003.
Values sent between devices are 32-bit elements; how exact they have to be, the bound alone decides.
No kernel may reach another device: no remote copies, remote signals or barrier semaphores. Data moves between devices by JAX's collectives and lax.ppermute only.
A program may use at most 32 MiB of HBM per device.

v0:
```python
import functools
import jax
import jax.numpy as jnp
from jax import lax
from jax.experimental import pallas as pl
from jax.experimental.pallas import tpu as pltpu
from jax.sharding import PartitionSpec as P

SOUND_SQUARED = 1.0
COURANT = 0.045
SHEAR_SPEED = 1.0
FIELDS = 8
NODES = (-1, 0, 1, 2)


def minmod_slope(backward, forward):
    smaller = jnp.where(jnp.abs(backward) < jnp.abs(forward), backward, forward)
    return jnp.where(backward * forward > 0.0, smaller, 0.0)


def physical_flux(state, normal):
    density, momentum, magnetic = state[0], state[1:4], state[4:7]
    inverse = 1.0 / density
    velocity = [m * inverse for m in momentum]
    normal_vel, normal_mag = velocity[normal], magnetic[normal]
    magnetic_sq = magnetic[0] * magnetic[0] + magnetic[1] * magnetic[1] + magnetic[2] * magnetic[2]
    momentum_flux = [m * normal_vel - b * normal_mag for m, b in zip(momentum, magnetic)]
    momentum_flux[normal] = momentum_flux[normal] + (SOUND_SQUARED * density + 0.5 * magnetic_sq)
    magnetic_flux = [b * normal_vel - v * normal_mag for b, v in zip(magnetic, velocity)]
    fluxes = [momentum[normal], *momentum_flux, *magnetic_flux, state[7] * normal_vel]
    return fluxes, jnp.abs(normal_vel) + jnp.sqrt(SOUND_SQUARED + magnetic_sq * inverse)


def face_flux(left, right, normal):
    left_flux, left_speed = physical_flux(left, normal)
    right_flux, right_speed = physical_flux(right, normal)
    half_speed = 0.5 * jnp.maximum(left_speed, right_speed)
    return [
        0.5 * (lf + rf) - half_speed * (r - l)
        for lf, rf, l, r in zip(left_flux, right_flux, left, right)
    ]


def faces_of(cells):
    lower, upper = [], []
    for back, here, ahead in zip(*cells):
        half = 0.5 * minmod_slope(here - back, ahead - here)
        lower.append(here - half)
        upper.append(here + half)
    return lower, upper


def line_difference(cells, normal):
    edges = [faces_of(cells[i - 1 : i + 2]) for i in range(1, len(cells) - 1)]
    fluxes = [face_flux(a[1], b[0], normal) for a, b in zip(edges[:-1], edges[1:])]
    return [[u - l for u, l in zip(*pair)] for pair in zip(fluxes[1:], fluxes[:-1])]


def pack_rows(block, first, ref):
    for layer in range(block.shape[1]):
        for field in range(FIELDS):
            tile = block[field, layer]
            ref[field, 2 * layer : 2 * layer + 2, :] = jnp.where(first, tile[:2], tile[-2:])


def emit_sends(rows, state_ref, odd_ref, even_ref, layers_ref, strip_ref):
    row = lax.axis_index("gx")
    even_row = row % 2 == 0
    even_column = lax.axis_index("gy") % 2 == 0
    low_end = (row == 0) | ((row != rows - 1) & even_row)
    state = state_ref[...]
    pack_rows(state, even_column, odd_ref)
    pack_rows(state, jnp.logical_not(even_column), even_ref)
    layers_ref[...] = jnp.where(even_row, state[:, -2:], state[:, :2])
    strip_ref[...] = jnp.where(low_end, state[:, :2], state[:, -2:])


def prepare(rows, density, velocity, magnetic, concentration, state_ref, *sends):
    mass = density[...]
    state_ref[0] = mass
    for i in range(3):
        state_ref[1 + i] = mass * velocity[i]
        state_ref[4 + i] = magnetic[i]
    state_ref[7] = mass * concentration[...]
    emit_sends(rows, state_ref, *sends)


def copy_all(pairs, done):
    copies = [pltpu.make_async_copy(a, b, done.at[i]) for i, (a, b) in enumerate(pairs)]
    for copy in copies:
        copy.start()
    for copy in copies:
        copy.wait()


def join_halves(strip, other_strip, payload):
    payload[0] = strip[...]
    payload[1] = other_strip[...]


def pick_other(layers, near, far, state, picked, done):
    pairs = [(near.at[1], picked.at[0]), (far.at[1], picked.at[1])]
    for k in range(layers // 2):
        pairs.append((state.at[:, 2 * k : 2 * k + 2], picked.at[2 + k]))
    copy_all(pairs, done)


def advance(
    section, rows, columns, cores, cells_ref, frac_ref, initial, state,
    near, far, passed_on, odd, even, across, *out
):
    result, strip_ref = out[0], out[-1]
    row, column, core = (lax.axis_index(axis) for axis in ("gx", "gy", "gz"))
    is_first, is_last = row == 0, row == rows - 1
    is_end = is_first | is_last
    even_row, even_column, low_core = row % 2 == 0, column % 2 == 0, core == 0
    layers, block_y, block_z = state.shape[1:]

    cells = cells_ref[section]
    blocks = lax.rem(lax.div(cells + 1, block_y) + columns - 1, columns)
    within = lax.rem(cells + 1, block_y)
    odd_shift = lax.rem(blocks, cores)
    start = jnp.where(
        is_first,
        block_y * (1 - odd_shift) + block_y - 1 - within,
        block_y * odd_shift + block_y - 2 + within,
    )
    fraction = frac_ref[section]
    weights = []
    for target in NODES:
        weight, scale = 1.0, 1.0
        for source in NODES:
            if source != target:
                weight = weight * (source - fraction)
                scale = scale * (source - target)
        weights.append(weight * (1.0 / scale))
    pieces = []
    for mine, passed in ((near[0], passed_on[0]), (far[0], passed_on[1])):
        pieces.append(jnp.where(low_core, mine, passed))
        pieces.append(jnp.where(low_core, passed, mine))
    for place in range(4):
        strip_ref[:, :, block_y * place : block_y * (place + 1), :] = jnp.where(
            is_first, pieces[3 - place], pieces[place]
        )
    ghost = 0.0
    for place in range(4):
        factor = jnp.where(is_first, weights[3 - place], weights[place])
        ghost = ghost + factor * strip_ref[:, :, pl.ds(start + place, block_y), :]
    push = jnp.where(is_first, SHEAR_SPEED, -SHEAR_SPEED)
    ghost = [ghost[f] + push * ghost[0] if f == 2 else ghost[f] for f in range(FIELDS)]
    below, above = [], []
    for f in range(FIELDS):
        inner = jnp.where(is_end, ghost[f], near[0, f])
        below.append(jnp.where(even_row, inner, across[f]))
        above.append(jnp.where(even_row, across[f], inner))

    line = [[below[f][i] for f in range(FIELDS)] for i in range(2)]
    line += [[state[f, i] for f in range(FIELDS)] for i in range(layers)]
    line += [[above[f][i] for f in range(FIELDS)] for i in range(2)]
    radial = line_difference(line, 0)

    before = [jnp.where(even_column, odd[f], even[f]) for f in range(FIELDS)]
    after = [jnp.where(even_column, even[f], odd[f]) for f in range(FIELDS)]
    y_index = lax.broadcasted_iota(jnp.int32, (block_y, block_z), 0)
    z_index = lax.broadcasted_iota(jnp.int32, (block_y, block_z), 1)
    for layer in range(layers):
        here = line[2 + layer]
        shifted = {0: here}
        for s in (1, 2):
            shifted[-s] = [
                jnp.where(
                    y_index < s,
                    pltpu.roll(before[f], (block_y - 2 * layer - 2 + s) % block_y, 0),
                    pltpu.roll(here[f], s, 0),
                )
                for f in range(FIELDS)
            ]
            shifted[s] = [
                jnp.where(
                    y_index >= block_y - s,
                    pltpu.roll(after[f], (block_y - s - 2 * layer) % block_y, 0),
                    pltpu.roll(here[f], block_y - s, 0),
                )
                for f in range(FIELDS)
            ]
        azimuthal = line_difference([shifted[s] for s in range(-2, 3)], 1)[0]
        beside = [passed_on[2 + layer // 2, f, layer % 2] for f in range(FIELDS)]
        for s in (1, 2):
            shifted[-s] = [
                jnp.where(z_index < s, pltpu.roll(beside[f], s, 1), pltpu.roll(here[f], s, 1))
                for f in range(FIELDS)
            ]
            shifted[s] = [
                jnp.where(
                    z_index >= block_z - s,
                    pltpu.roll(beside[f], block_z - s, 1),
                    pltpu.roll(here[f], block_z - s, 1),
                )
                for f in range(FIELDS)
            ]
        vertical = line_difference([shifted[s] for s in range(-2, 3)], 2)[0]
        for f in range(FIELDS):
            stepped = here[f] - COURANT * (radial[layer][f] + azimuthal[f] + vertical[f])
            if section == 1:
                stepped = 0.5 * initial[f, layer] + 0.5 * stepped
            result[f, layer] = stepped
    if section == 0:
        emit_sends(rows, result, *out[1:5])


def swaps(pairs):
    return [(a, b) for a, b in pairs] + [(b, a) for a, b in pairs]


def sheared_route(step):
    rows, columns, cores = (lax.axis_size(axis) for axis in ("gx", "gy", "gz"))
    place = lambda i, j, c: (i * columns + j % columns) * cores + c
    pairs = []
    for j in range(columns):
        for c in range(cores):
            pairs.append((place(rows - 1, j, c), place(0, j + cores * step + c, c)))
            pairs += [(place(i, j, c), place(i + 1, j, c)) for i in range(1, rows - 2, 2)]
    return swaps(pairs)


def other_core(block):
    return lax.ppermute(block, "gz", [(0, 1), (1, 0)])


def exchange(step, steps):
    def branch(operands):
        payload, odd_rows, even_rows, even_layers = operands
        everywhere = ("gx", "gy", "gz")
        near = lax.ppermute(payload, everywhere, sheared_route(step))
        far = lax.ppermute(payload, everywhere, sheared_route((step + 1) % steps))
        columns = lax.axis_size("gy")
        odd = lax.ppermute(
            odd_rows, "gy", swaps([(i, (i + 1) % columns) for i in range(1, columns, 2)])
        )
        even = lax.ppermute(even_rows, "gy", swaps([(i, i + 1) for i in range(0, columns, 2)]))
        layers = lax.ppermute(
            even_layers, "gx", swaps([(i, i + 1) for i in range(0, lax.axis_size("gx"), 2)])
        )
        return near, far, odd, even, layers

    return branch


def body(density, velocity, magnetic, concentration, shear_cells, shear_frac):
    layers, block_y, block_z = density.shape
    rows, columns, cores = (lax.axis_size(axis) for axis in ("gx", "gy", "gz"))
    shape = lambda *dims: jax.ShapeDtypeStruct(dims, jnp.float32)
    state_shape = shape(FIELDS, layers, block_y, block_z)
    packed = shape(FIELDS, 2 * layers, block_z)
    edge = shape(FIELDS, 2, block_y, block_z)
    sends = [packed, packed, edge, edge]
    whole = pl.BlockSpec(memory_space=pltpu.VMEM)
    scalars = pl.BlockSpec(memory_space=pltpu.SMEM)
    anywhere = pl.BlockSpec(memory_space=pl.ANY)
    initial, *messages, strip = pl.pallas_call(
        functools.partial(prepare, rows),
        out_shape=[state_shape, *sends],
        in_specs=[whole] * 4,
        out_specs=[whole] * 5,
        name="prepare",
    )(density, velocity, magnetic, concentration)
    steps = columns // cores
    state = initial
    for section in range(2):
        payload = pl.pallas_call(
            join_halves,
            out_shape=shape(2, *edge.shape),
            in_specs=[whole] * 2,
            out_specs=whole,
            name="payload",
        )(strip, other_core(strip))
        blocks = ((shear_cells[section] + 1) // block_y - 1) % columns
        near, far, *rest = lax.switch(
            blocks // cores, [exchange(n, steps) for n in range(steps)], (payload, *messages)
        )
        pieces = 2 + layers // 2
        picked = pl.pallas_call(
            functools.partial(pick_other, layers),
            out_shape=shape(pieces, *edge.shape),
            in_specs=[anywhere] * 3,
            out_specs=whole,
            scratch_shapes=[pltpu.SemaphoreType.DMA((pieces,))],
            name="pick",
        )(near, far, state)
        passed = other_core(picked)
        out = [state_shape, *sends] if section == 0 else [state_shape]
        advanced = pl.pallas_call(
            functools.partial(advance, section, rows, columns, cores),
            out_shape=out,
            in_specs=[scalars] * 2 + [whole] * 8,
            out_specs=[whole] * len(out),
            scratch_shapes=[pltpu.VMEM((FIELDS, 2, 4 * block_y, block_z), jnp.float32)],
            compiler_params=pltpu.CompilerParams(vmem_limit_bytes=16 * 1024 * 1024),
            name="advance",
        )(shear_cells, shear_frac, initial, state, near, far, passed, *rest)
        if section == 0:
            state, *messages, strip = advanced
    return advanced[0]


def solution(mesh):
    placed = (
        P("gx", "gy", "gz"),
        P(None, "gx", "gy", "gz"),
        P(None, "gx", "gy", "gz"),
        P("gx", "gy", "gz"),
        P(),
        P(),
    )
    return jax.shard_map(
        body, mesh=mesh, in_specs=placed, out_specs=P(None, "gx", "gy", "gz"), check_vma=False
    )
```

profile of v0, /device:TPU:17, one launch (start us, length us, event | category | flops | bytes accessed | tf_op | source)
XLA Modules:
  0.0 114.5 jit_solution(10824112539743076177)
XLA Ops:
  1.6 2.7 %collective-permute-start.320 = (f32[8,2,8,128]{3,2,1,0:T(8,128)}, f32[8,2,8,128]{3,2,1,0:T(8,128)S(1)}, u32[]{:S(2)}, u32[]{:S(2)}) collective-permute-start(f32[8,2,8,128]{3,2,1,0:T(8,128)} %get-tuple-element.794.strip), channel_id=1, source_target_pairs={{0,1},{1,0},{2,3},{3,2},{4,5},{5,4},{6,7},{7,6},{8,9},{9,8},{10,11... | collective-permute-start | bytes 196616 | tf_op jit(solution)/shard_map/ppermute | solution.py:227
  7.1 38.4 %conditional.2 = (f32[2,8,2,8,128]{4,3,2,1,0:T(8,128)}, f32[2,8,2,8,128]{4,3,2,1,0:T(8,128)}, f32[8,8,128]{2,1,0:T(8,128)}, f32[8,8,128]{2,1,0:T(8,128)}, f32[8,2,8,128]{3,2,1,0:T(8,128)}) conditional(s32[]{:T(128)} %clamp.6, (f32[2,8,2,8,128]{4,3,2,1,0:T(8,128)S(1)}, f32[8,8,128]{2,1,0:T(8,128)S(1)}, ...), branch_computations={%region_0.1_spmd, %region_1.2_spmd, %region_2.3_spmd, %region_3.4_... | conditional | bytes 1573104 | solution.py:278
  7.2 21.3 %collective-permute-start.16 = (f32[2,8,2,8,128]{4,3,2,1,0:T(8,128)S(1)}, f32[2,8,2,8,128]{4,3,2,1,0:T(8,128)}, u32[]{:S(2)}, u32[]{:S(2)}) collective-permute-start(f32[2,8,2,8,128]{4,3,2,1,0:T(8,128)S(1)} %get-tuple-element.529), channel_id=1, source_target_pairs={{896,16},{128,256},{384,512},{640,768},{897,19},{129,257},{385,513... | collective-permute-start | bytes 393224 | tf_op jit(solution)/shard_map/cond/branch_3_fun/ppermute | solution.py:235
  28.5 1.9 %collective-permute-start.15 = (f32[2,8,2,8,128]{4,3,2,1,0:T(8,128)S(1)}, f32[2,8,2,8,128]{4,3,2,1,0:T(8,128)}, u32[]{:S(2)}, u32[]{:S(2)}) collective-permute-start(f32[2,8,2,8,128]{4,3,2,1,0:T(8,128)S(1)} %get-tuple-element.529), channel_id=1, source_target_pairs={{896,12},{128,256},{384,512},{640,768},{897,15},{129,257},{385,513... | collective-permute-start | bytes 393224 | tf_op jit(solution)/shard_map/cond/branch_3_fun/ppermute | solution.py:234
  30.4 1.9 %collective-permute-start.19 = (f32[8,2,8,128]{3,2,1,0:T(8,128)S(1)}, f32[8,2,8,128]{3,2,1,0:T(8,128)}, u32[]{:S(2)}, u32[]{:S(2)}) collective-permute-start(f32[8,2,8,128]{3,2,1,0:T(8,128)S(1)} %get-tuple-element.532), channel_id=1, source_target_pairs={{0,128},{256,384},{512,640},{768,896},{128,0},{384,256},{640,512},... | collective-permute-start | bytes 196616 | tf_op jit(solution)/shard_map/cond/branch_3_fun/ppermute | solution.py:241
  32.3 3.4 %collective-permute-start.17 = (f32[8,8,128]{2,1,0:T(8,128)S(1)}, f32[8,8,128]{2,1,0:T(8,128)}, u32[]{:S(2)}, u32[]{:S(2)}) collective-permute-start(f32[8,8,128]{2,1,0:T(8,128)S(1)} %get-tuple-element.530), channel_id=1, source_target_pairs={{2,4},{6,8},{10,12},{14,16},{18,20},{22,24},{26,28},{30,32},{34,36... | collective-permute-start | bytes 98312 | tf_op jit(solution)/shard_map/cond/branch_3_fun/ppermute | solution.py:237
  35.7 1.9 %collective-permute-start.18 = (f32[8,8,128]{2,1,0:T(8,128)S(1)}, f32[8,8,128]{2,1,0:T(8,128)}, u32[]{:S(2)}, u32[]{:S(2)}) collective-permute-start(f32[8,8,128]{2,1,0:T(8,128)S(1)} %get-tuple-element.531), channel_id=1, source_target_pairs={{0,2},{4,6},{8,10},{12,14},{16,18},{20,22},{24,26},{28,30},{32,34}... | collective-permute-start | bytes 98312 | tf_op jit(solution)/shard_map/cond/branch_3_fun/ppermute | solution.py:240
  37.7 1.8 %collective-permute-done.17 = f32[8,8,128]{2,1,0:T(8,128)} collective-permute-done((f32[8,8,128]{2,1,0:T(8,128)S(1)}, f32[8,8,128]{2,1,0:T(8,128)}, u32[]{:S(2)}, u32[]{:S(2)}) %collective-permute-start.17) | collective-permute-done | bytes 32800 | tf_op jit(solution)/shard_map/cond/branch_3_fun/ppermute | solution.py:237
  40.5 5.0 %collective-permute-done.15 = f32[2,8,2,8,128]{4,3,2,1,0:T(8,128)} collective-permute-done((f32[2,8,2,8,128]{4,3,2,1,0:T(8,128)S(1)}, f32[2,8,2,8,128]{4,3,2,1,0:T(8,128)}, u32[]{:S(2)}, u32[]{:S(2)}) %collective-permute-start.15) | collective-permute-done | bytes 131104 | tf_op jit(solution)/shard_map/cond/branch_3_fun/ppermute | solution.py:234
  45.5 1.7 %pick.2 = f32[4,8,2,8,128]{4,3,2,1,0:T(8,128)} custom-call(f32[2,8,2,8,128]{4,3,2,1,0:T(8,128)} %get-tuple-element.798.near, f32[2,8,2,8,128]{4,3,2,1,0:T(8,128)} %get-tuple-element.799.far, f32[8,4,8,128]{3,2,1,0:T(8,128)} %get-tuple-element.793.state.initial), custom_call_target="tpu_custom_call" | custom-call | tf_op jit(solution)/shard_map/pick/pallas_call | solution.py:282
  47.3 1.9 %collective-permute-start.321 = (f32[4,8,2,8,128]{4,3,2,1,0:T(8,128)}, f32[4,8,2,8,128]{4,3,2,1,0:T(8,128)S(1)}, u32[]{:S(2)}, u32[]{:S(2)}) collective-permute-start(f32[4,8,2,8,128]{4,3,2,1,0:T(8,128)} %pick.2), channel_id=1, source_target_pairs={{0,1},{1,0},{2,3},{3,2},{4,5},{5,4},{6,7},{7,6},{8,9},{9,8},{10,11... | collective-permute-start | bytes 786440 | tf_op jit(solution)/shard_map/ppermute | solution.py:227
  51.6 2.0 %advance.2 = (f32[8,4,8,128]{3,2,1,0:T(8,128)S(1)}, f32[8,8,128]{2,1,0:T(8,128)S(1)}, f32[8,8,128]{2,1,0:T(8,128)S(1)}, f32[8,2,8,128]{3,2,1,0:T(8,128)S(1)}, f32[8,2,8,128]{3,2,1,0:T(8,128)S(1)}) custom-call(s32[2]{0:T(128)S(1)} %copy-done.4, f32[2]{0:T(128)S(1)} %copy-done.5, f32[8,4,8,128]{3,2,1,0:T(8,128)S(1)} %copy-done, f32[8,4,8,128]{3,2,1,0:T(8,128)S(1)} %copy-done, ...), custom_call_target="tpu_custom_call" | custom-call | tf_op jit(solution)/shard_map/advance/pallas_call | solution.py:292
  54.3 2.0 %collective-permute-start.322 = (f32[8,2,8,128]{3,2,1,0:T(8,128)S(1)}, f32[8,2,8,128]{3,2,1,0:T(8,128)S(1)}, u32[]{:S(2)}, u32[]{:S(2)}) collective-permute-start(f32[8,2,8,128]{3,2,1,0:T(8,128)S(1)} %get-tuple-element.804.strip), channel_id=1, source_target_pairs={{0,1},{1,0},{2,3},{3,2},{4,5},{5,4},{6,7},{7,6},{8,9},{9,8},{10,11... | collective-permute-start | bytes 196616 | tf_op jit(solution)/shard_map/ppermute | solution.py:227
  58.9 36.3 %conditional.3 = (f32[2,8,2,8,128]{4,3,2,1,0:T(8,128)}, f32[2,8,2,8,128]{4,3,2,1,0:T(8,128)}, f32[8,8,128]{2,1,0:T(8,128)}, f32[8,8,128]{2,1,0:T(8,128)}, f32[8,2,8,128]{3,2,1,0:T(8,128)}) conditional(s32[]{:T(128)} %clamp.7, (f32[2,8,2,8,128]{4,3,2,1,0:T(8,128)S(1)}, f32[8,8,128]{2,1,0:T(8,128)S(1)}, ...), branch_computations={%region_32.33_spmd, %region_33.34_spmd, %region_34.35_spmd, %regio... | conditional | bytes 1573104 | solution.py:278
  59.0 8.5 %collective-permute-start.296 = (f32[2,8,2,8,128]{4,3,2,1,0:T(8,128)S(1)}, f32[2,8,2,8,128]{4,3,2,1,0:T(8,128)}, u32[]{:S(2)}, u32[]{:S(2)}) collective-permute-start(f32[2,8,2,8,128]{4,3,2,1,0:T(8,128)S(1)} %get-tuple-element.753), channel_id=1, source_target_pairs={{896,112},{128,256},{384,512},{640,768},{897,115},{129,257},{385,5... | collective-permute-start | bytes 393224 | tf_op jit(solution)/shard_map/cond/branch_27_fun/ppermute | solution.py:235
  67.5 9.9 %collective-permute-start.295 = (f32[2,8,2,8,128]{4,3,2,1,0:T(8,128)S(1)}, f32[2,8,2,8,128]{4,3,2,1,0:T(8,128)}, u32[]{:S(2)}, u32[]{:S(2)}) collective-permute-start(f32[2,8,2,8,128]{4,3,2,1,0:T(8,128)S(1)} %get-tuple-element.753), channel_id=1, source_target_pairs={{896,108},{128,256},{384,512},{640,768},{897,111},{129,257},{385,5... | collective-permute-start | bytes 393224 | tf_op jit(solution)/shard_map/cond/branch_27_fun/ppermute | solution.py:234
  77.4 1.9 %collective-permute-start.299 = (f32[8,2,8,128]{3,2,1,0:T(8,128)S(1)}, f32[8,2,8,128]{3,2,1,0:T(8,128)}, u32[]{:S(2)}, u32[]{:S(2)}) collective-permute-start(f32[8,2,8,128]{3,2,1,0:T(8,128)S(1)} %get-tuple-element.756), channel_id=1, source_target_pairs={{0,128},{256,384},{512,640},{768,896},{128,0},{384,256},{640,512},... | collective-permute-start | bytes 196616 | tf_op jit(solution)/shard_map/cond/branch_27_fun/ppermute | solution.py:241
  79.3 5.9 %collective-permute-start.297 = (f32[8,8,128]{2,1,0:T(8,128)S(1)}, f32[8,8,128]{2,1,0:T(8,128)}, u32[]{:S(2)}, u32[]{:S(2)}) collective-permute-start(f32[8,8,128]{2,1,0:T(8,128)S(1)} %get-tuple-element.754), channel_id=1, source_target_pairs={{2,4},{6,8},{10,12},{14,16},{18,20},{22,24},{26,28},{30,32},{34,36... | collective-permute-start | bytes 98312 | tf_op jit(solution)/shard_map/cond/branch_27_fun/ppermute | solution.py:237
  85.3 1.9 %collective-permute-start.298 = (f32[8,8,128]{2,1,0:T(8,128)S(1)}, f32[8,8,128]{2,1,0:T(8,128)}, u32[]{:S(2)}, u32[]{:S(2)}) collective-permute-start(f32[8,8,128]{2,1,0:T(8,128)S(1)} %get-tuple-element.755), channel_id=1, source_target_pairs={{0,2},{4,6},{8,10},{12,14},{16,18},{20,22},{24,26},{28,30},{32,34}... | collective-permute-start | bytes 98312 | tf_op jit(solution)/shard_map/cond/branch_27_fun/ppermute | solution.py:240
  87.2 2.8 %collective-permute-done.298 = f32[8,8,128]{2,1,0:T(8,128)} collective-permute-done((f32[8,8,128]{2,1,0:T(8,128)S(1)}, f32[8,8,128]{2,1,0:T(8,128)}, u32[]{:S(2)}, u32[]{:S(2)}) %collective-permute-start.298) | collective-permute-done | bytes 32800 | tf_op jit(solution)/shard_map/cond/branch_27_fun/ppermute | solution.py:240
  90.1 5.2 %collective-permute-done.295 = f32[2,8,2,8,128]{4,3,2,1,0:T(8,128)} collective-permute-done((f32[2,8,2,8,128]{4,3,2,1,0:T(8,128)S(1)}, f32[2,8,2,8,128]{4,3,2,1,0:T(8,128)}, u32[]{:S(2)}, u32[]{:S(2)}) %collective-permute-start.295) | collective-permute-done | bytes 131104 | tf_op jit(solution)/shard_map/cond/branch_27_fun/ppermute | solution.py:234
  95.2 1.7 %pick.3 = f32[4,8,2,8,128]{4,3,2,1,0:T(8,128)} custom-call(f32[2,8,2,8,128]{4,3,2,1,0:T(8,128)} %get-tuple-element.808.near, f32[2,8,2,8,128]{4,3,2,1,0:T(8,128)} %get-tuple-element.809.far, f32[8,4,8,128]{3,2,1,0:T(8,128)} %copy-done.1), custom_call_target="tpu_custom_call" | custom-call | tf_op jit(solution)/shard_map/pick/pallas_call | solution.py:282
  97.0 13.5 %collective-permute-start.323 = (f32[4,8,2,8,128]{4,3,2,1,0:T(8,128)}, f32[4,8,2,8,128]{4,3,2,1,0:T(8,128)S(1)}, u32[]{:S(2)}, u32[]{:S(2)}) collective-permute-start(f32[4,8,2,8,128]{4,3,2,1,0:T(8,128)} %pick.3), channel_id=1, source_target_pairs={{0,1},{1,0},{2,3},{3,2},{4,5},{5,4},{6,7},{7,6},{8,9},{9,8},{10,11... | collective-permute-start | bytes 786440 | tf_op jit(solution)/shard_map/ppermute | solution.py:227
  111.8 2.7 %advance.3 = f32[8,4,8,128]{3,2,1,0:T(8,128)} custom-call(s32[2]{0:T(128)S(1)} %copy-done.4, f32[2]{0:T(128)S(1)} %copy-done.5, f32[8,4,8,128]{3,2,1,0:T(8,128)S(1)} %copy-done, f32[8,4,8,128]{3,2,1,0:T(8,128)S(1)} %copy-done.2, f32[2,8,2,8,128]{4,3,2,1,0:T(8,128)} %get-tuple-element.808.near, f32[2,8,2,8,128]{4,3,2,1,0:T(8,128)} %get-tuple-element.809.far, ...), custom_call_target="tpu_custom_call" | custom-call | tf_op jit(solution)/shard_map/advance/pallas_call | solution.py:292
  (30 shorter events, 11.0 us)
Async XLA Ops:
  1.6 2.7 %copy-start.4 = (s32[2]{0:T(128)S(1)}, s32[2]{0:T(128)}, u32[]{:S(2)}) copy-start(s32[2]{0:T(128)} %cells_ref.3) | copy-start | bytes 28
  1.6 4.1 %collective-permute-start.320 = (f32[8,2,8,128]{3,2,1,0:T(8,128)}, f32[8,2,8,128]{3,2,1,0:T(8,128)S(1)}, u32[]{:S(2)}, u32[]{:S(2)}) collective-permute-start(f32[8,2,8,128]{3,2,1,0:T(8,128)} %get-tuple-element.794.strip), channel_id=1, source_target_pairs={{0,1},{1,0},{2,3},{3,2},{4,5},{5,4},{6,7},{7,6},{8,9},{9,8},{10,11... | collective-permute-start | bytes 196616 | tf_op jit(solution)/shard_map/ppermute | solution.py:227
  5.6 0.6 copy-start.7
  7.2 33.3 %collective-permute-start.16 = (f32[2,8,2,8,128]{4,3,2,1,0:T(8,128)S(1)}, f32[2,8,2,8,128]{4,3,2,1,0:T(8,128)}, u32[]{:S(2)}, u32[]{:S(2)}) collective-permute-start(f32[2,8,2,8,128]{4,3,2,1,0:T(8,128)S(1)} %get-tuple-element.529), channel_id=1, source_target_pairs={{896,16},{128,256},{384,512},{640,768},{897,19},{129,257},{385,513... | collective-permute-start | bytes 393224 | tf_op jit(solution)/shard_map/cond/branch_3_fun/ppermute | solution.py:235
  28.5 17.0 %collective-permute-start.15 = (f32[2,8,2,8,128]{4,3,2,1,0:T(8,128)S(1)}, f32[2,8,2,8,128]{4,3,2,1,0:T(8,128)}, u32[]{:S(2)}, u32[]{:S(2)}) collective-permute-start(f32[2,8,2,8,128]{4,3,2,1,0:T(8,128)S(1)} %get-tuple-element.529), channel_id=1, source_target_pairs={{896,12},{128,256},{384,512},{640,768},{897,15},{129,257},{385,513... | collective-permute-start | bytes 393224 | tf_op jit(solution)/shard_map/cond/branch_3_fun/ppermute | solution.py:234
  30.4 10.1 %collective-permute-start.19 = (f32[8,2,8,128]{3,2,1,0:T(8,128)S(1)}, f32[8,2,8,128]{3,2,1,0:T(8,128)}, u32[]{:S(2)}, u32[]{:S(2)}) collective-permute-start(f32[8,2,8,128]{3,2,1,0:T(8,128)S(1)} %get-tuple-element.532), channel_id=1, source_target_pairs={{0,128},{256,384},{512,640},{768,896},{128,0},{384,256},{640,512},... | collective-permute-start | bytes 196616 | tf_op jit(solution)/shard_map/cond/branch_3_fun/ppermute | solution.py:241
  32.3 7.1 %collective-permute-start.17 = (f32[8,8,128]{2,1,0:T(8,128)S(1)}, f32[8,8,128]{2,1,0:T(8,128)}, u32[]{:S(2)}, u32[]{:S(2)}) collective-permute-start(f32[8,8,128]{2,1,0:T(8,128)S(1)} %get-tuple-element.530), channel_id=1, source_target_pairs={{2,4},{6,8},{10,12},{14,16},{18,20},{22,24},{26,28},{30,32},{34,36... | collective-permute-start | bytes 98312 | tf_op jit(solution)/shard_map/cond/branch_3_fun/ppermute | solution.py:237
  35.7 4.8 %collective-permute-start.18 = (f32[8,8,128]{2,1,0:T(8,128)S(1)}, f32[8,8,128]{2,1,0:T(8,128)}, u32[]{:S(2)}, u32[]{:S(2)}) collective-permute-start(f32[8,8,128]{2,1,0:T(8,128)S(1)} %get-tuple-element.531), channel_id=1, source_target_pairs={{0,2},{4,6},{8,10},{12,14},{16,18},{20,22},{24,26},{28,30},{32,34}... | collective-permute-start | bytes 98312 | tf_op jit(solution)/shard_map/cond/branch_3_fun/ppermute | solution.py:240
  45.5 5.4 %copy-start = (f32[8,4,8,128]{3,2,1,0:T(8,128)S(1)}, f32[8,4,8,128]{3,2,1,0:T(8,128)}, u32[]{:S(2)}) copy-start(f32[8,4,8,128]{3,2,1,0:T(8,128)} %get-tuple-element.793.state.initial) | copy-start | bytes 393220
  47.3 3.6 %collective-permute-start.321 = (f32[4,8,2,8,128]{4,3,2,1,0:T(8,128)}, f32[4,8,2,8,128]{4,3,2,1,0:T(8,128)S(1)}, u32[]{:S(2)}, u32[]{:S(2)}) collective-permute-start(f32[4,8,2,8,128]{4,3,2,1,0:T(8,128)} %pick.2), channel_id=1, source_target_pairs={{0,1},{1,0},{2,3},{3,2},{4,5},{5,4},{6,7},{7,6},{8,9},{9,8},{10,11... | collective-permute-start | bytes 786440 | tf_op jit(solution)/shard_map/ppermute | solution.py:227
  50.9 0.7 copy-start.5
  53.6 0.7 copy-start.1
  54.3 3.1 %copy-start.3 = (f32[8,2,8,128]{3,2,1,0:T(8,128)}, f32[8,2,8,128]{3,2,1,0:T(8,128)S(1)}, u32[]{:S(2)}) copy-start(f32[8,2,8,128]{3,2,1,0:T(8,128)S(1)} %get-tuple-element.804.strip) | copy-start | bytes 196612
  54.3 3.1 %collective-permute-start.322 = (f32[8,2,8,128]{3,2,1,0:T(8,128)S(1)}, f32[8,2,8,128]{3,2,1,0:T(8,128)S(1)}, u32[]{:S(2)}, u32[]{:S(2)}) collective-permute-start(f32[8,2,8,128]{3,2,1,0:T(8,128)S(1)} %get-tuple-element.804.strip), channel_id=1, source_target_pairs={{0,1},{1,0},{2,3},{3,2},{4,5},{5,4},{6,7},{7,6},{8,9},{9,8},{10,11... | collective-permute-start | bytes 196616 | tf_op jit(solution)/shard_map/ppermute | solution.py:227
  57.4 0.6 copy-start.6
  59.0 31.1 %collective-permute-start.296 = (f32[2,8,2,8,128]{4,3,2,1,0:T(8,128)S(1)}, f32[2,8,2,8,128]{4,3,2,1,0:T(8,128)}, u32[]{:S(2)}, u32[]{:S(2)}) collective-permute-start(f32[2,8,2,8,128]{4,3,2,1,0:T(8,128)S(1)} %get-tuple-element.753), channel_id=1, source_target_pairs={{896,112},{128,256},{384,512},{640,768},{897,115},{129,257},{385,5... | collective-permute-start | bytes 393224 | tf_op jit(solution)/shard_map/cond/branch_27_fun/ppermute | solution.py:235
  67.5 27.8 %collective-permute-start.295 = (f32[2,8,2,8,128]{4,3,2,1,0:T(8,128)S(1)}, f32[2,8,2,8,128]{4,3,2,1,0:T(8,128)}, u32[]{:S(2)}, u32[]{:S(2)}) collective-permute-start(f32[2,8,2,8,128]{4,3,2,1,0:T(8,128)S(1)} %get-tuple-element.753), channel_id=1, source_target_pairs={{896,108},{128,256},{384,512},{640,768},{897,111},{129,257},{385,5... | collective-permute-start | bytes 393224 | tf_op jit(solution)/shard_map/cond/branch_27_fun/ppermute | solution.py:234
  77.4 12.7 %collective-permute-start.299 = (f32[8,2,8,128]{3,2,1,0:T(8,128)S(1)}, f32[8,2,8,128]{3,2,1,0:T(8,128)}, u32[]{:S(2)}, u32[]{:S(2)}) collective-permute-start(f32[8,2,8,128]{3,2,1,0:T(8,128)S(1)} %get-tuple-element.756), channel_id=1, source_target_pairs={{0,128},{256,384},{512,640},{768,896},{128,0},{384,256},{640,512},... | collective-permute-start | bytes 196616 | tf_op jit(solution)/shard_map/cond/branch_27_fun/ppermute | solution.py:241
  79.3 7.9 %collective-permute-start.297 = (f32[8,8,128]{2,1,0:T(8,128)S(1)}, f32[8,8,128]{2,1,0:T(8,128)}, u32[]{:S(2)}, u32[]{:S(2)}) collective-permute-start(f32[8,8,128]{2,1,0:T(8,128)S(1)} %get-tuple-element.754), channel_id=1, source_target_pairs={{2,4},{6,8},{10,12},{14,16},{18,20},{22,24},{26,28},{30,32},{34,36... | collective-permute-start | bytes 98312 | tf_op jit(solution)/shard_map/cond/branch_27_fun/ppermute | solution.py:237
  85.3 4.8 %collective-permute-start.298 = (f32[8,8,128]{2,1,0:T(8,128)S(1)}, f32[8,8,128]{2,1,0:T(8,128)}, u32[]{:S(2)}, u32[]{:S(2)}) collective-permute-start(f32[8,8,128]{2,1,0:T(8,128)S(1)} %get-tuple-element.755), channel_id=1, source_target_pairs={{0,2},{4,6},{8,10},{12,14},{16,18},{20,22},{24,26},{28,30},{32,34}... | collective-permute-start | bytes 98312 | tf_op jit(solution)/shard_map/cond/branch_27_fun/ppermute | solution.py:240
  95.2 16.6 %copy-start.2 = (f32[8,4,8,128]{3,2,1,0:T(8,128)S(1)}, f32[8,4,8,128]{3,2,1,0:T(8,128)}, u32[]{:S(2)}) copy-start(f32[8,4,8,128]{3,2,1,0:T(8,128)} %copy-done.1) | copy-start | bytes 393220
  97.0 14.8 %collective-permute-start.323 = (f32[4,8,2,8,128]{4,3,2,1,0:T(8,128)}, f32[4,8,2,8,128]{4,3,2,1,0:T(8,128)S(1)}, u32[]{:S(2)}, u32[]{:S(2)}) collective-permute-start(f32[4,8,2,8,128]{4,3,2,1,0:T(8,128)} %pick.3), channel_id=1, source_target_pairs={{0,1},{1,0},{2,3},{3,2},{4,5},{5,4},{6,7},{7,6},{8,9},{9,8},{10,11... | collective-permute-start | bytes 786440 | tf_op jit(solution)/shard_map/ppermute | solution.py:227
where the time goes:
time: 115 us; the launch traced here: 114 us
  starting transfers between devices  78.8 us (69%)
  waiting for transfers between devices  19.3 us (17%)
  Pallas kernels  11.5 us (10%)
  local copies, waits for them, and re-layouts  3.22 us (3%)
  between operations  1.52 us (1%)
    ppermute x2, starting transfers between devices, branch(): far = lax.ppermute(payload, everywhere, sheared_route((step + 1) % steps))  29.8 us
    ppermute x4, starting transfers between devices, other_core(): return lax.ppermute(block, 'gz', [(0, 1), (1, 0)])  20.1 us
    ppermute x2, starting transfers between devices, branch(): near = lax.ppermute(payload, everywhere, sheared_route(step))  11.8 us
    ppermute x2, waiting for transfers between devices, branch(): near = lax.ppermute(payload, everywhere, sheared_route(step))  10.2 us
    ppermute x2, starting transfers between devices, branch(): lax.ppermute(odd_rows, 'gy', swaps([(i, (i + 1) % columns) for i in range...  9.33 us
    pallas_call x2, Pallas kernels, body(): pl.pallas_call(functools.partial(advance, section, rows, columns, cores),...  4.73 us
    ppermute x2, waiting for transfers between devices, branch(): lax.ppermute(even_rows, 'gy', swaps([(i, i + 1) for i in range(0, columns...  3.85 us
    ppermute x2, starting transfers between devices, branch(): lax.ppermute(even_layers, 'gx', swaps([(i, i + 1) for i in range(0, lax.a...  3.84 us
  transfers between devices with their start and end apart: 14, of which 8 were waited for; matrix products, arithmetic and copies ran while one was open for 1% of the time, Pallas kernels for 0%

commit v1 on v0

--- a/solution.py
+++ b/solution.py
@@ -257,11 +257,13 @@
     whole = pl.BlockSpec(memory_space=pltpu.VMEM)
     scalars = pl.BlockSpec(memory_space=pltpu.SMEM)
     anywhere = pl.BlockSpec(memory_space=pl.ANY)
+    small = pltpu.CompilerParams(vmem_limit_bytes=4 * 1024 * 1024)
     initial, *messages, strip = pl.pallas_call(
         functools.partial(prepare, rows),
         out_shape=[state_shape, *sends],
         in_specs=[whole] * 4,
         out_specs=[whole] * 5,
+        compiler_params=small,
         name="prepare",
     )(density, velocity, magnetic, concentration)
     steps = columns // cores
@@ -272,6 +274,7 @@
             out_shape=shape(2, *edge.shape),
             in_specs=[whole] * 2,
             out_specs=whole,
+            compiler_params=small,
             name="payload",
         )(strip, other_core(strip))
         blocks = ((shear_cells[section] + 1) // block_y - 1) % columns
@@ -285,6 +288,7 @@
             in_specs=[anywhere] * 3,
             out_specs=whole,
             scratch_shapes=[pltpu.SemaphoreType.DMA((pieces,))],
+            compiler_params=small,
             name="pick",
         )(near, far, state)
         passed = other_core(picked)
@@ -295,7 +299,7 @@
             in_specs=[scalars] * 2 + [whole] * 8,
             out_specs=[whole] * len(out),
             scratch_shapes=[pltpu.VMEM((FIELDS, 2, 4 * block_y, block_z), jnp.float32)],
-            compiler_params=pltpu.CompilerParams(vmem_limit_bytes=16 * 1024 * 1024),
+            compiler_params=pltpu.CompilerParams(vmem_limit_bytes=8 * 1024 * 1024),
             name="advance",
         )(shear_cells, shear_frac, initial, state, near, far, passed, *rest)
         if section == 0:

time: 115 us -> 115 us (level)
  the two profiles are of different devices: /device:TPU:17 before, /device:TPU:31 now
where the time goes in v1:
time: 115 us
  starting transfers between devices  83.7 us (73%)
  waiting for transfers between devices  18 us (16%)
  Pallas kernels  6.57 us (6%)
  local copies, waits for them, and re-layouts  4.27 us (4%)
  between operations  1.57 us (1%)
    ppermute x2, starting transfers between devices, branch(): far = lax.ppermute(payload, everywhere, sheared_route((step + 1) % steps))  29.3 us
    ppermute x2, starting transfers between devices, branch(): lax.ppermute(odd_rows, 'gy', swaps([(i, (i + 1) % columns) for i in range...  17.1 us
    ppermute x2, starting transfers between devices, branch(): near = lax.ppermute(payload, everywhere, sheared_route(step))  17 us
    ppermute x2, waiting for transfers between devices, branch(): lax.ppermute(odd_rows, 'gy', swaps([(i, (i + 1) % columns) for i in range...  15.5 us
    ppermute x4, starting transfers between devices, other_core(): return lax.ppermute(block, 'gz', [(0, 1), (1, 0)])  12.7 us
    pallas_call x2, Pallas kernels, body(): pl.pallas_call(functools.partial(advance, section, rows, columns, cores),...  4.69 us
    ppermute x2, starting transfers between devices, branch(): lax.ppermute(even_layers, 'gx', swaps([(i, i + 1) for i in range(0, lax.a...  3.84 us
    ppermute x2, starting transfers between devices, branch(): lax.ppermute(even_rows, 'gy', swaps([(i, i + 1) for i in range(0, columns...  3.84 us
  transfers between devices with their start and end apart: 14, of which 5 were waited for; matrix products, arithmetic and copies ran while one was open for 1% of the time, Pallas kernels for 0%

profile of v1, /device:TPU:31, one launch (start us, length us, event | category | flops | bytes accessed | tf_op | source)
XLA Modules:
  0.0 114.5 jit_solution(9082788431759240976)
XLA Ops:
  3.1 2.6 %collective-permute-start.320 = (f32[8,2,8,128]{3,2,1,0:T(8,128)S(1)}, f32[8,2,8,128]{3,2,1,0:T(8,128)S(1)}, u32[]{:S(2)}, u32[]{:S(2)}) collective-permute-start(f32[8,2,8,128]{3,2,1,0:T(8,128)S(1)} %get-tuple-element.794.strip), channel_id=1, source_target_pairs={{0,1},{1,0},{2,3},{3,2},{4,5},{5,4},{6,7},{7,6},{8,9},{9,8},{10,11... | collective-permute-start | bytes 196616 | tf_op jit(solution)/shard_map/ppermute | solution.py:227
  7.0 48.0 %conditional.2 = (f32[2,8,2,8,128]{4,3,2,1,0:T(8,128)}, f32[2,8,2,8,128]{4,3,2,1,0:T(8,128)}, f32[8,8,128]{2,1,0:T(8,128)}, f32[8,8,128]{2,1,0:T(8,128)}, f32[8,2,8,128]{3,2,1,0:T(8,128)}) conditional(s32[]{:T(128)} %clamp.6, (f32[2,8,2,8,128]{4,3,2,1,0:T(8,128)S(1)}, f32[8,8,128]{2,1,0:T(8,128)S(1)}, ...), branch_computations={%region_0.1_spmd, %region_1.2_spmd, %region_2.3_spmd, %region_3.4_... | conditional | bytes 1573104 | solution.py:281
  7.1 24.8 %collective-permute-start.86 = (f32[2,8,2,8,128]{4,3,2,1,0:T(8,128)S(1)}, f32[2,8,2,8,128]{4,3,2,1,0:T(8,128)}, u32[]{:S(2)}, u32[]{:S(2)}) collective-permute-start(f32[2,8,2,8,128]{4,3,2,1,0:T(8,128)S(1)} %get-tuple-element.585), channel_id=1, source_target_pairs={{896,72},{128,256},{384,512},{640,768},{897,75},{129,257},{385,513... | collective-permute-start | bytes 393224 | tf_op jit(solution)/shard_map/cond/branch_17_fun/ppermute | solution.py:235
  31.9 2.9 %collective-permute-start.85 = (f32[2,8,2,8,128]{4,3,2,1,0:T(8,128)S(1)}, f32[2,8,2,8,128]{4,3,2,1,0:T(8,128)}, u32[]{:S(2)}, u32[]{:S(2)}) collective-permute-start(f32[2,8,2,8,128]{4,3,2,1,0:T(8,128)S(1)} %get-tuple-element.585), channel_id=1, source_target_pairs={{896,68},{128,256},{384,512},{640,768},{897,71},{129,257},{385,513... | collective-permute-start | bytes 393224 | tf_op jit(solution)/shard_map/cond/branch_17_fun/ppermute | solution.py:234
  34.8 1.9 %collective-permute-start.89 = (f32[8,2,8,128]{3,2,1,0:T(8,128)S(1)}, f32[8,2,8,128]{3,2,1,0:T(8,128)}, u32[]{:S(2)}, u32[]{:S(2)}) collective-permute-start(f32[8,2,8,128]{3,2,1,0:T(8,128)S(1)} %get-tuple-element.588), channel_id=1, source_target_pairs={{0,128},{256,384},{512,640},{768,896},{128,0},{384,256},{640,512},... | collective-permute-start | bytes 196616 | tf_op jit(solution)/shard_map/cond/branch_17_fun/ppermute | solution.py:241
  36.8 12.7 %collective-permute-start.87 = (f32[8,8,128]{2,1,0:T(8,128)S(1)}, f32[8,8,128]{2,1,0:T(8,128)}, u32[]{:S(2)}, u32[]{:S(2)}) collective-permute-start(f32[8,8,128]{2,1,0:T(8,128)S(1)} %get-tuple-element.586), channel_id=1, source_target_pairs={{2,4},{6,8},{10,12},{14,16},{18,20},{22,24},{26,28},{30,32},{34,36... | collective-permute-start | bytes 98312 | tf_op jit(solution)/shard_map/cond/branch_17_fun/ppermute | solution.py:237
  49.5 1.9 %collective-permute-start.88 = (f32[8,8,128]{2,1,0:T(8,128)S(1)}, f32[8,8,128]{2,1,0:T(8,128)}, u32[]{:S(2)}, u32[]{:S(2)}) collective-permute-start(f32[8,8,128]{2,1,0:T(8,128)S(1)} %get-tuple-element.587), channel_id=1, source_target_pairs={{0,2},{4,6},{8,10},{12,14},{16,18},{20,22},{24,26},{28,30},{32,34}... | collective-permute-start | bytes 98312 | tf_op jit(solution)/shard_map/cond/branch_17_fun/ppermute | solution.py:240
  51.4 3.4 %collective-permute-done.87 = f32[8,8,128]{2,1,0:T(8,128)} collective-permute-done((f32[8,8,128]{2,1,0:T(8,128)S(1)}, f32[8,8,128]{2,1,0:T(8,128)}, u32[]{:S(2)}, u32[]{:S(2)}) %collective-permute-start.87) | collective-permute-done | bytes 32800 | tf_op jit(solution)/shard_map/cond/branch_17_fun/ppermute | solution.py:237
  55.1 0.9 pick.2
  56.0 4.0 %collective-permute-start.321 = (f32[4,8,2,8,128]{4,3,2,1,0:T(8,128)S(1)}, f32[4,8,2,8,128]{4,3,2,1,0:T(8,128)S(1)}, u32[]{:S(2)}, u32[]{:S(2)}) collective-permute-start(f32[4,8,2,8,128]{4,3,2,1,0:T(8,128)S(1)} %pick.2), channel_id=1, source_target_pairs={{0,1},{1,0},{2,3},{3,2},{4,5},{5,4},{6,7},{7,6},{8,9},{9,8},{10,11... | collective-permute-start | bytes 786440 | tf_op jit(solution)/shard_map/ppermute | solution.py:227
  60.0 1.1 collective-permute-done.321.passed_on
  61.8 2.0 %advance.2 = (f32[8,4,8,128]{3,2,1,0:T(8,128)S(1)}, f32[8,8,128]{2,1,0:T(8,128)S(1)}, f32[8,8,128]{2,1,0:T(8,128)S(1)}, f32[8,2,8,128]{3,2,1,0:T(8,128)S(1)}, f32[8,2,8,128]{3,2,1,0:T(8,128)S(1)}) custom-call(s32[2]{0:T(128)S(1)} %copy-done.4, f32[2]{0:T(128)S(1)} %copy-done.5, f32[8,4,8,128]{3,2,1,0:T(8,128)S(1)} %get-tuple-element.793.state.initial, ...), custom_call_target="tpu_custom_call" | custom-call | tf_op jit(solution)/shard_map/advance/pallas_call | solution.py:296
  63.8 2.3 %collective-permute-start.322 = (f32[8,2,8,128]{3,2,1,0:T(8,128)S(1)}, f32[8,2,8,128]{3,2,1,0:T(8,128)S(1)}, u32[]{:S(2)}, u32[]{:S(2)}) collective-permute-start(f32[8,2,8,128]{3,2,1,0:T(8,128)S(1)} %get-tuple-element.804.strip), channel_id=1, source_target_pairs={{0,1},{1,0},{2,3},{3,2},{4,5},{5,4},{6,7},{7,6},{8,9},{9,8},{10,11... | collective-permute-start | bytes 196616 | tf_op jit(solution)/shard_map/ppermute | solution.py:227
  67.0 38.9 %conditional.3 = (f32[2,8,2,8,128]{4,3,2,1,0:T(8,128)}, f32[2,8,2,8,128]{4,3,2,1,0:T(8,128)}, f32[8,8,128]{2,1,0:T(8,128)}, f32[8,8,128]{2,1,0:T(8,128)}, f32[8,2,8,128]{3,2,1,0:T(8,128)}) conditional(s32[]{:T(128)} %clamp.7, (f32[2,8,2,8,128]{4,3,2,1,0:T(8,128)S(1)}, f32[8,8,128]{2,1,0:T(8,128)S(1)}, ...), branch_computations={%region_32.33_spmd, %region_33.34_spmd, %region_34.35_spmd, %regio... | conditional | bytes 1573104 | solution.py:281
  67.0 4.5 %collective-permute-start.176 = (f32[2,8,2,8,128]{4,3,2,1,0:T(8,128)S(1)}, f32[2,8,2,8,128]{4,3,2,1,0:T(8,128)}, u32[]{:S(2)}, u32[]{:S(2)}) collective-permute-start(f32[2,8,2,8,128]{4,3,2,1,0:T(8,128)S(1)} %get-tuple-element.657), channel_id=1, source_target_pairs={{896,16},{128,256},{384,512},{640,768},{897,19},{129,257},{385,513... | collective-permute-start | bytes 393224 | tf_op jit(solution)/shard_map/cond/branch_3_fun/ppermute | solution.py:235
  71.6 14.1 %collective-permute-start.175 = (f32[2,8,2,8,128]{4,3,2,1,0:T(8,128)S(1)}, f32[2,8,2,8,128]{4,3,2,1,0:T(8,128)}, u32[]{:S(2)}, u32[]{:S(2)}) collective-permute-start(f32[2,8,2,8,128]{4,3,2,1,0:T(8,128)S(1)} %get-tuple-element.657), channel_id=1, source_target_pairs={{896,12},{128,256},{384,512},{640,768},{897,15},{129,257},{385,513... | collective-permute-start | bytes 393224 | tf_op jit(solution)/shard_map/cond/branch_3_fun/ppermute | solution.py:234
  85.6 1.9 %collective-permute-start.179 = (f32[8,2,8,128]{3,2,1,0:T(8,128)S(1)}, f32[8,2,8,128]{3,2,1,0:T(8,128)}, u32[]{:S(2)}, u32[]{:S(2)}) collective-permute-start(f32[8,2,8,128]{3,2,1,0:T(8,128)S(1)} %get-tuple-element.660), channel_id=1, source_target_pairs={{0,128},{256,384},{512,640},{768,896},{128,0},{384,256},{640,512},... | collective-permute-start | bytes 196616 | tf_op jit(solution)/shard_map/cond/branch_3_fun/ppermute | solution.py:241
  87.6 4.3 %collective-permute-start.177 = (f32[8,8,128]{2,1,0:T(8,128)S(1)}, f32[8,8,128]{2,1,0:T(8,128)}, u32[]{:S(2)}, u32[]{:S(2)}) collective-permute-start(f32[8,8,128]{2,1,0:T(8,128)S(1)} %get-tuple-element.658), channel_id=1, source_target_pairs={{2,4},{6,8},{10,12},{14,16},{18,20},{22,24},{26,28},{30,32},{34,36... | collective-permute-start | bytes 98312 | tf_op jit(solution)/shard_map/cond/branch_3_fun/ppermute | solution.py:237
  91.9 1.9 %collective-permute-start.178 = (f32[8,8,128]{2,1,0:T(8,128)S(1)}, f32[8,8,128]{2,1,0:T(8,128)}, u32[]{:S(2)}, u32[]{:S(2)}) collective-permute-start(f32[8,8,128]{2,1,0:T(8,128)S(1)} %get-tuple-element.659), channel_id=1, source_target_pairs={{0,2},{4,6},{8,10},{12,14},{16,18},{20,22},{24,26},{28,30},{32,34}... | collective-permute-start | bytes 98312 | tf_op jit(solution)/shard_map/cond/branch_3_fun/ppermute | solution.py:240
  93.8 12.1 %collective-permute-done.177 = f32[8,8,128]{2,1,0:T(8,128)} collective-permute-done((f32[8,8,128]{2,1,0:T(8,128)S(1)}, f32[8,8,128]{2,1,0:T(8,128)}, u32[]{:S(2)}, u32[]{:S(2)}) %collective-permute-start.177) | collective-permute-done | bytes 32800 | tf_op jit(solution)/shard_map/cond/branch_3_fun/ppermute | solution.py:237
  106.0 0.9 pick.3
  106.9 3.8 %collective-permute-start.323 = (f32[4,8,2,8,128]{4,3,2,1,0:T(8,128)S(1)}, f32[4,8,2,8,128]{4,3,2,1,0:T(8,128)S(1)}, u32[]{:S(2)}, u32[]{:S(2)}) collective-permute-start(f32[4,8,2,8,128]{4,3,2,1,0:T(8,128)S(1)} %pick.3), channel_id=1, source_target_pairs={{0,1},{1,0},{2,3},{3,2},{4,5},{5,4},{6,7},{7,6},{8,9},{9,8},{10,11... | collective-permute-start | bytes 786440 | tf_op jit(solution)/shard_map/ppermute | solution.py:227
  110.7 1.1 collective-permute-done.323.passed_on
  111.8 2.7 %advance.3 = f32[8,4,8,128]{3,2,1,0:T(8,128)} custom-call(s32[2]{0:T(128)S(1)} %copy-done.4, f32[2]{0:T(128)S(1)} %copy-done.5, f32[8,4,8,128]{3,2,1,0:T(8,128)S(1)} %get-tuple-element.793.state.initial, f32[8,4,8,128]{3,2,1,0:T(8,128)S(1)} %get-tuple-element.803.state, f32[2,8,2,8,128]{4,3,2,1,0:T(8,128)} %get-tuple-element.808.near, ...), custom_call_target="tpu_custom_call" | custom-call | tf_op jit(solution)/shard_map/advance/pallas_call | solution.py:296
  (26 shorter events, 4.5 us)
Async XLA Ops:
  0.0 0.8 copy-start
  0.8 0.8 copy-start.1
  1.6 0.7 copy-start.2
  2.3 0.7 copy-start.3
  3.1 2.6 %copy-start.4 = (s32[2]{0:T(128)S(1)}, s32[2]{0:T(128)}, u32[]{:S(2)}) copy-start(s32[2]{0:T(128)} %cells_ref.3) | copy-start | bytes 28
  3.1 3.9 %collective-permute-start.320 = (f32[8,2,8,128]{3,2,1,0:T(8,128)S(1)}, f32[8,2,8,128]{3,2,1,0:T(8,128)S(1)}, u32[]{:S(2)}, u32[]{:S(2)}) collective-permute-start(f32[8,2,8,128]{3,2,1,0:T(8,128)S(1)} %get-tuple-element.794.strip), channel_id=1, source_target_pairs={{0,1},{1,0},{2,3},{3,2},{4,5},{5,4},{6,7},{7,6},{8,9},{9,8},{10,11... | collective-permute-start | bytes 196616 | tf_op jit(solution)/shard_map/ppermute | solution.py:227
  7.1 47.8 %collective-permute-start.86 = (f32[2,8,2,8,128]{4,3,2,1,0:T(8,128)S(1)}, f32[2,8,2,8,128]{4,3,2,1,0:T(8,128)}, u32[]{:S(2)}, u32[]{:S(2)}) collective-permute-start(f32[2,8,2,8,128]{4,3,2,1,0:T(8,128)S(1)} %get-tuple-element.585), channel_id=1, source_target_pairs={{896,72},{128,256},{384,512},{640,768},{897,75},{129,257},{385,513... | collective-permute-start | bytes 393224 | tf_op jit(solution)/shard_map/cond/branch_17_fun/ppermute | solution.py:235
  31.9 23.0 %collective-permute-start.85 = (f32[2,8,2,8,128]{4,3,2,1,0:T(8,128)S(1)}, f32[2,8,2,8,128]{4,3,2,1,0:T(8,128)}, u32[]{:S(2)}, u32[]{:S(2)}) collective-permute-start(f32[2,8,2,8,128]{4,3,2,1,0:T(8,128)S(1)} %get-tuple-element.585), channel_id=1, source_target_pairs={{896,68},{128,256},{384,512},{640,768},{897,71},{129,257},{385,513... | collective-permute-start | bytes 393224 | tf_op jit(solution)/shard_map/cond/branch_17_fun/ppermute | solution.py:234
  34.8 20.0 %collective-permute-start.89 = (f32[8,2,8,128]{3,2,1,0:T(8,128)S(1)}, f32[8,2,8,128]{3,2,1,0:T(8,128)}, u32[]{:S(2)}, u32[]{:S(2)}) collective-permute-start(f32[8,2,8,128]{3,2,1,0:T(8,128)S(1)} %get-tuple-element.588), channel_id=1, source_target_pairs={{0,128},{256,384},{512,640},{768,896},{128,0},{384,256},{640,512},... | collective-permute-start | bytes 196616 | tf_op jit(solution)/shard_map/cond/branch_17_fun/ppermute | solution.py:241
  36.8 18.1 %collective-permute-start.87 = (f32[8,8,128]{2,1,0:T(8,128)S(1)}, f32[8,8,128]{2,1,0:T(8,128)}, u32[]{:S(2)}, u32[]{:S(2)}) collective-permute-start(f32[8,8,128]{2,1,0:T(8,128)S(1)} %get-tuple-element.586), channel_id=1, source_target_pairs={{2,4},{6,8},{10,12},{14,16},{18,20},{22,24},{26,28},{30,32},{34,36... | collective-permute-start | bytes 98312 | tf_op jit(solution)/shard_map/cond/branch_17_fun/ppermute | solution.py:237
  49.5 5.4 %collective-permute-start.88 = (f32[8,8,128]{2,1,0:T(8,128)S(1)}, f32[8,8,128]{2,1,0:T(8,128)}, u32[]{:S(2)}, u32[]{:S(2)}) collective-permute-start(f32[8,8,128]{2,1,0:T(8,128)S(1)} %get-tuple-element.587), channel_id=1, source_target_pairs={{0,2},{4,6},{8,10},{12,14},{16,18},{20,22},{24,26},{28,30},{32,34}... | collective-permute-start | bytes 98312 | tf_op jit(solution)/shard_map/cond/branch_17_fun/ppermute | solution.py:240
  56.0 5.1 %collective-permute-start.321 = (f32[4,8,2,8,128]{4,3,2,1,0:T(8,128)S(1)}, f32[4,8,2,8,128]{4,3,2,1,0:T(8,128)S(1)}, u32[]{:S(2)}, u32[]{:S(2)}) collective-permute-start(f32[4,8,2,8,128]{4,3,2,1,0:T(8,128)S(1)} %pick.2), channel_id=1, source_target_pairs={{0,1},{1,0},{2,3},{3,2},{4,5},{5,4},{6,7},{7,6},{8,9},{9,8},{10,11... | collective-permute-start | bytes 786440 | tf_op jit(solution)/shard_map/ppermute | solution.py:227
  61.1 0.7 copy-start.5
  63.8 3.2 %collective-permute-start.322 = (f32[8,2,8,128]{3,2,1,0:T(8,128)S(1)}, f32[8,2,8,128]{3,2,1,0:T(8,128)S(1)}, u32[]{:S(2)}, u32[]{:S(2)}) collective-permute-start(f32[8,2,8,128]{3,2,1,0:T(8,128)S(1)} %get-tuple-element.804.strip), channel_id=1, source_target_pairs={{0,1},{1,0},{2,3},{3,2},{4,5},{5,4},{6,7},{7,6},{8,9},{9,8},{10,11... | collective-permute-start | bytes 196616 | tf_op jit(solution)/shard_map/ppermute | solution.py:227
  67.0 38.9 %collective-permute-start.176 = (f32[2,8,2,8,128]{4,3,2,1,0:T(8,128)S(1)}, f32[2,8,2,8,128]{4,3,2,1,0:T(8,128)}, u32[]{:S(2)}, u32[]{:S(2)}) collective-permute-start(f32[2,8,2,8,128]{4,3,2,1,0:T(8,128)S(1)} %get-tuple-element.657), channel_id=1, source_target_pairs={{896,16},{128,256},{384,512},{640,768},{897,19},{129,257},{385,513... | collective-permute-start | bytes 393224 | tf_op jit(solution)/shard_map/cond/branch_3_fun/ppermute | solution.py:235
  71.6 34.4 %collective-permute-start.175 = (f32[2,8,2,8,128]{4,3,2,1,0:T(8,128)S(1)}, f32[2,8,2,8,128]{4,3,2,1,0:T(8,128)}, u32[]{:S(2)}, u32[]{:S(2)}) collective-permute-start(f32[2,8,2,8,128]{4,3,2,1,0:T(8,128)S(1)} %get-tuple-element.657), channel_id=1, source_target_pairs={{896,12},{128,256},{384,512},{640,768},{897,15},{129,257},{385,513... | collective-permute-start | bytes 393224 | tf_op jit(solution)/shard_map/cond/branch_3_fun/ppermute | solution.py:234
  85.6 20.3 %collective-permute-start.179 = (f32[8,2,8,128]{3,2,1,0:T(8,128)S(1)}, f32[8,2,8,128]{3,2,1,0:T(8,128)}, u32[]{:S(2)}, u32[]{:S(2)}) collective-permute-start(f32[8,2,8,128]{3,2,1,0:T(8,128)S(1)} %get-tuple-element.660), channel_id=1, source_target_pairs={{0,128},{256,384},{512,640},{768,896},{128,0},{384,256},{640,512},... | collective-permute-start | bytes 196616 | tf_op jit(solution)/shard_map/cond/branch_3_fun/ppermute | solution.py:241
  87.6 18.4 %collective-permute-start.177 = (f32[8,8,128]{2,1,0:T(8,128)S(1)}, f32[8,8,128]{2,1,0:T(8,128)}, u32[]{:S(2)}, u32[]{:S(2)}) collective-permute-start(f32[8,8,128]{2,1,0:T(8,128)S(1)} %get-tuple-element.658), channel_id=1, source_target_pairs={{2,4},{6,8},{10,12},{14,16},{18,20},{22,24},{26,28},{30,32},{34,36... | collective-permute-start | bytes 98312 | tf_op jit(solution)/shard_map/cond/branch_3_fun/ppermute | solution.py:237
  91.9 14.0 %collective-permute-start.178 = (f32[8,8,128]{2,1,0:T(8,128)S(1)}, f32[8,8,128]{2,1,0:T(8,128)}, u32[]{:S(2)}, u32[]{:S(2)}) collective-permute-start(f32[8,8,128]{2,1,0:T(8,128)S(1)} %get-tuple-element.659), channel_id=1, source_target_pairs={{0,2},{4,6},{8,10},{12,14},{16,18},{20,22},{24,26},{28,30},{32,34}... | collective-permute-start | bytes 98312 | tf_op jit(solution)/shard_map/cond/branch_3_fun/ppermute | solution.py:240
  106.9 4.9 %collective-permute-start.323 = (f32[4,8,2,8,128]{4,3,2,1,0:T(8,128)S(1)}, f32[4,8,2,8,128]{4,3,2,1,0:T(8,128)S(1)}, u32[]{:S(2)}, u32[]{:S(2)}) collective-permute-start(f32[4,8,2,8,128]{4,3,2,1,0:T(8,128)S(1)} %pick.3), channel_id=1, source_target_pairs={{0,1},{1,0},{2,3},{3,2},{4,5},{5,4},{6,7},{7,6},{8,9},{9,8},{10,11... | collective-permute-start | bytes 786440 | tf_op jit(solution)/shard_map/ppermute | solution.py:227
